TPU v7x, 32 devices: a whole 2x2x4 slice. The times are simulated.
32 devices in a mesh: wave: 8 (over y, x, core), lev: 4 (over z).
Axes of the slice: x: 2, y: 2, z: 4, core: 2. Of those that a mesh axis runs over, the one named last changes fastest.
Arguments:
- vort_div: float32 [4, 4, 80, 80], P(None, 'lev', 'wave'), may hold values from -0.4 to 0.4
- legendre: float32 [80, 8, 80], P('wave'), may hold values from -1 to 1
- owner_map: int32 [80], replicated, may hold values from 0 to 79, as said below
- lat_sine: float32 [8], P('wave'), may hold values from -0.9 to 0.9
- quad_weight: float32 [8], P('wave'), may hold values from 2 to 6
- thickness: float32 [4], P('lev'), may hold values from 0.02 to 0.08
- tracers: float32 [8, 4, 8, 160], P(None, 'lev', 'wave'), may hold values from -6 to 6
Outputs:
- tendency: float32 [8, 2, 4, 80, 80], P(None, None, 'lev', 'wave')
Inputs may be any that keep to these rules, and one draw needn't show every extreme that they name: `owner_map`: a permutation of the 80 wavenumbers in which slots 2 i and 2 i + 1 hold m and 79 - m.
All inputs are finite; a program needn't handle non-finite values.
Results may differ from a plain program's by a relative error of at most 0.00007.
Values sent between devices are 32-bit elements; how exact they have to be, the bound alone decides.
A program may use at most 64 MiB of HBM per device.

v0:
```python
import math

import jax
import jax.numpy as jnp
from jax import lax
from jax.sharding import PartitionSpec as P

planet_radius = 20.0


def prefix_2(shard, axis, combine, identity):
    count, place = (lax.axis_size(axis), lax.axis_index(axis))
    everything = lax.all_gather(shard, axis)
    start = jnp.broadcast_to(jnp.asarray(identity, shard.dtype), shard.shape)

    def hop(k, before):
        reached = k < place
        new = combine(before, everything[k])
        return jnp.where(reached, new, before)

    return lax.fori_loop(0, count, hop, start)


def with_halo(shard, sides, width):
    for axis, dim in sides:
        count, length = (lax.axis_size(axis), shard.shape[dim])
        up = [(i, (i + 1) % count) for i in range(count - 1)]
        down = [(j, i) for i, j in up]
        last = lax.slice_in_dim(shard, length - width, length, axis=dim)
        initial = lax.slice_in_dim(shard, 0, width, axis=dim)
        before = lax.ppermute(last, axis, up)
        after = lax.ppermute(initial, axis, down)
        shard = jnp.concatenate([before, shard, after], axis=dim)
    return shard


def spectral_winds(vort_div, wavenumbers, degrees):
    order = wavenumbers.astype(jnp.float32)[:, None]
    degree = jnp.arange(degrees).astype(jnp.float32)[None, :]
    ratio = jnp.maximum(degree * degree - order * order, 0.0) / jnp.maximum(
        4.0 * degree * degree - 1.0, 1.0
    )
    coupling = jnp.where(degree > order, jnp.sqrt(ratio), 0.0)
    inverse = jnp.where(
        degree > 0, -planet_radius * planet_radius / jnp.maximum(degree * (degree + 1.0), 1.0), 0.0
    )
    coupling_next = jnp.concatenate(
        [coupling[:, 1:], jnp.zeros((coupling.shape[0], 1), jnp.float32)], axis=1
    )

    def derivative(field):
        edge = jnp.zeros(field.shape[:-1] + (1,), jnp.float32)
        lower = jnp.concatenate([edge, field[..., :-1]], axis=-1)
        upper = jnp.concatenate([field[..., 1:], edge], axis=-1)
        return -(degree - 1.0) * coupling * lower + (degree + 2.0) * coupling_next * upper

    stream_real = inverse * vort_div[0]
    stream_imag = inverse * vort_div[1]
    potential_real = inverse * vort_div[2]
    potential_imag = inverse * vort_div[3]
    east_real = (-order * potential_imag - derivative(stream_real)) / planet_radius
    east_imag = (order * potential_real - derivative(stream_imag)) / planet_radius
    north_real = (-order * stream_imag + derivative(potential_real)) / planet_radius
    north_imag = (order * stream_real + derivative(potential_imag)) / planet_radius
    return jnp.stack(
        [east_real, east_imag, north_real, north_imag, vort_div[2], vort_div[3]], axis=0
    )


def matmul(left, right):
    return jnp.dot(left, right, precision=lax.Precision.HIGHEST, preferred_element_type=jnp.float32)


def block_width(length):
    widest = min(512, length)
    for candidate in range(widest, 0, -1):
        if length % candidate == 0:
            return candidate
    return 1


def angle_tables(wavenumbers, length, width):
    offsets = jnp.arange(width, dtype=jnp.int32)
    product = wavenumbers[:, None] * offsets[None, :] % length
    angles = product.astype(jnp.float32) * (2.0 * math.pi / length)
    return (jnp.cos(angles), jnp.sin(angles))


def block_phase(wavenumbers, length, start):
    angles = (wavenumbers * start % length).astype(jnp.float32) * (2.0 * math.pi / length)
    return (jnp.cos(angles), jnp.sin(angles))


def to_grid(real_part, imag_part, tables, wavenumbers, length, width):
    cosines, sines = tables
    pieces = []
    for block in range(length // width):
        phase_cos, phase_sin = block_phase(wavenumbers, length, block * width)
        turned_real = real_part * phase_cos - imag_part * phase_sin
        turned_imag = real_part * phase_sin + imag_part * phase_cos
        pieces.append(matmul(turned_real, cosines) - matmul(turned_imag, sines))
    return jnp.concatenate(pieces, axis=1)


def to_spectrum(values, tables, wavenumbers, length, width):
    cosines, sines = tables
    cos_total = jnp.zeros((values.shape[0], wavenumbers.shape[0]), jnp.float32)
    sin_total = jnp.zeros((values.shape[0], wavenumbers.shape[0]), jnp.float32)
    for block in range(length // width):
        segment = values[:, block * width : (block + 1) * width]
        along_cos = matmul(segment, cosines.T)
        along_sin = matmul(segment, sines.T)
        phase_cos, phase_sin = block_phase(wavenumbers, length, block * width)
        cos_total = cos_total + phase_cos * along_cos - phase_sin * along_sin
        sin_total = sin_total + phase_sin * along_cos + phase_cos * along_sin
    scale = 2.0 / length
    return (scale * cos_total, -scale * sin_total)


def shards(vort_div, legendre, owner_map, lat_sine, quad_weight, thickness, tracers):
    slots, lat_total, degrees = legendre.shape
    length = tracers.shape[3]
    levels = tracers.shape[1]
    lat_rows = tracers.shape[2]
    tracer_count = tracers.shape[0]
    wavenumber_total = owner_map.shape[0]
    own_orders = lax.dynamic_slice_in_dim(owner_map, lax.axis_index("wave") * slots, slots)
    order = own_orders.astype(jnp.float32)[:, None]
    degree = jnp.arange(degrees).astype(jnp.float32)[None, :]
    valid = degree >= order
    coefficients = jnp.where(valid, spectral_winds(vort_div, own_orders, degrees), 0.0)
    fourier = jnp.einsum(
        "sjn,fksn->fkjs",
        legendre,
        coefficients,
        precision=lax.Precision.HIGHEST,
        preferred_element_type=jnp.float32,
    )
    fourier = fourier.reshape(3, 2, levels, lat_total, slots)
    width = block_width(length)
    tables = angle_tables(owner_map, length, width)
    pieces = lax.all_to_all(fourier, "wave", split_axis=3, concat_axis=4, tiled=True)
    field_count = pieces.shape[0]
    real_part = pieces[:, 0].reshape(-1, wavenumber_total)
    imag_part = pieces[:, 1].reshape(-1, wavenumber_total)
    values = to_grid(real_part, imag_part, tables, owner_map, length, width)
    grid_fields = values.reshape(field_count, levels, lat_rows, length)
    east = grid_fields[0]
    north = grid_fields[1]
    divergence = grid_fields[2]
    layer_mass = divergence * thickness[:, None, None]
    running = jnp.cumsum(layer_mass, axis=0)
    column_total = running[-1]
    prefix = prefix_2(column_total, "lev", jnp.add, jnp.zeros_like(column_total))
    column = prefix[None] + running
    omega_bottom = -column
    omega_top = layer_mass - column
    merid_extended = with_halo(north * tracers, (("wave", 2),), 1)
    level_extended = with_halo(tracers, (("lev", 1),), 1)
    above = level_extended[:, :-2]
    below = level_extended[:, 2:]
    vertical = (
        omega_bottom * (tracers + below) * 0.5 - omega_top * (above + tracers) * 0.5
    ) / thickness[:, None, None]
    lon_step = 2.0 * math.pi / length
    lat_step = math.pi / wavenumber_total
    zonal_flux = east * tracers
    zonal = (jnp.roll(zonal_flux, -1, axis=3) - jnp.roll(zonal_flux, 1, axis=3)) / (2.0 * lon_step)
    merid = (merid_extended[:, :, 2:] - merid_extended[:, :, :-2]) / (2.0 * lat_step)
    metric = (1.0 - lat_sine * lat_sine)[None, None, :, None]
    grid_tendency = -quad_weight[None, None, :, None] * ((zonal + merid) / metric + vertical)
    cos_part, sin_part = to_spectrum(
        grid_tendency.reshape(-1, length), tables, owner_map, length, width
    )
    shape_out = (tracer_count, levels, lat_rows, wavenumber_total)
    spectra = jnp.stack([cos_part.reshape(shape_out), sin_part.reshape(shape_out)], axis=1)
    result = jnp.einsum(
        "sjn,crkjs->crksn",
        legendre,
        lax.all_to_all(spectra, "wave", split_axis=4, concat_axis=3, tiled=True),
        precision=lax.Precision.HIGHEST,
        preferred_element_type=jnp.float32,
    )
    return jnp.where(valid, result, 0.0)


def solution(mesh):
    placed = (
        P(None, "lev", "wave", None),
        P("wave", None, None),
        P(),
        P("wave"),
        P("wave"),
        P("lev"),
        P(None, "lev", "wave", None),
    )
    return jax.shard_map(
        shards,
        mesh=mesh,
        in_specs=placed,
        out_specs=P(None, None, "lev", "wave", None),
        check_vma=False,
    )
```

profile of v0, /device:TPU:0, one launch (start us, length us, event | category | flops | bytes accessed | tf_op | source)
XLA Modules:
  0.0 46.4 jit_solution(59143235062635799)
XLA Ops:
  0.0 0.1 slice.104
  0.1 0.7 %copy-done.3 = s32[80]{0:T(128)S(1)} copy-done((s32[80]{0:T(128)S(1)}, s32[80]{0:T(128)}, u32[]{:S(2)}) %copy-start.3) | copy-done | bytes 344
  0.8 0.1 fusion.72
  0.9 0.1 broadcast_compare_fusion
  0.9 0.1 slice.102
  1.0 0.1 slice.103
  1.1 0.7 %slice-done = f32[2,1,10,80]{3,1,2,0:T(1,128)S(1)} async-done(((f32[4,1,10,80]{3,1,2,0:T(1,128)}), f32[2,1,10,80]{3,1,2,0:T(1,128)S(1)}, s32[]{:S(2)}) %slice-start) | async-done | bytes 6424 | tf_op jit(solution)/shard_map/slice | solution.py:59
  1.8 0.1 copy-done.1
  1.9 0.1 sqrt_select_fusion
  2.0 0.1 fusion.76
  2.1 0.1 add_multiply_fusion.1
  2.2 0.1 fusion.75
  2.3 0.1 fusion.77
  2.4 0.1 subtract_multiply_fusion
  2.5 0.1 stack.14
  2.6 0.0 copy-done
  2.6 0.2 convolution_bitcast_fusion.1
  2.8 0.1 copy.44
  2.9 0.6 %copy.45 = f32[3,2,1,8,10]{4,1,0,2,3:T(2,128)} copy(f32[3,2,1,8,10]{4,3,1,0,2:T(8,128)S(1)} %bitcast.93) | data formatting | bytes 3840 | tf_op jit(solution)/shard_map/reshape | solution.py:139
  3.5 5.3 %all-to-all-start = ((f32[3,2,1,8,10]{4,1,0,2,3:T(2,128)}), f32[3,2,1,8,10]{4,1,0,2,3:T(2,128)S(1)}, u32[]{:S(2)}, u32[]{:S(2)}) async-start(f32[3,2,1,8,10]{4,1,0,2,3:T(2,128)} %copy.45), calls=%async_computation | async-start | bytes 49152 | tf_op jit(solution)/shard_map/all_to_all | solution.py:142
  8.8 1.3 %collective-permute-start.2 = (f32[8,1,1,160]{3,2,1,0:T(1,128)S(1)}, f32[8,1,1,160]{3,2,1,0:T(1,128)S(1)}, u32[]{:S(2)}, u32[]{:S(2)}) collective-permute-start(f32[8,1,1,160]{3,2,1,0:T(1,128)S(1)} %copy-done.2), channel_id=1, source_target_pairs={{1,0},{2,1},{3,2},{5,4},{6,5},{7,6},{9,8},{10,9},{11,10},{13,12},{... | collective-permute-start | bytes 15368 | tf_op jit(solution)/shard_map/ppermute | solution.py:32
  10.1 4.5 %collective-permute-start.3 = (f32[8,1,1,160]{3,2,1,0:T(1,128)S(1)}, f32[8,1,1,160]{3,2,1,0:T(1,128)S(1)}, u32[]{:S(2)}, u32[]{:S(2)}) collective-permute-start(f32[8,1,1,160]{3,2,1,0:T(1,128)S(1)} %copy-done.2), channel_id=1, source_target_pairs={{0,1},{1,2},{2,3},{4,5},{5,6},{6,7},{8,9},{9,10},{10,11},{12,13},{... | collective-permute-start | bytes 15368 | tf_op jit(solution)/shard_map/ppermute | solution.py:31
  16.6 0.0 all-to-all-done
  16.7 0.1 all_to_all.7
  16.8 0.5 %fusion.11 = f32[3,160]{1,0:T(4,128)S(1)} fusion(s32[80]{0:T(128)S(1)} %copy-done.3, f32[3,1,1,1,80]{4,1,0,3,2:T(1,128)S(1)} %get-tuple-element.140, f32[3,1,1,1,80]{4,1,0,3,2:T(1,128)S(1)} %get-tuple-element.139), kind=kOutput, calls=%fused_computation.17 | convolution fusion | flops 576480 | bytes 4160 | tf_op jit(solution)/shard_map/dot_general | solution.py:71
  17.3 0.5 %convolution_subtract_fusion = f32[3,160]{1,0:T(4,128)S(1)} fusion(f32[3,160]{1,0:T(4,128)S(1)} %fusion.11, s32[80]{0:T(128)S(1)} %copy-done.3, f32[3,1,1,1,80]{4,1,0,3,2:T(1,128)S(1)} %get-tuple-element.140, f32[3,1,1,1,80]{4,1,0,3,2:T(1,128)S(1)} %get-tuple-element.139), kind=kOutput, calls=%fused_computation.6 | convolution fusion | flops 576960 | bytes 6080 | tf_op jit(solution)/shard_map/dot_general | solution.py:71
  17.9 0.1 fusion.74
  17.9 0.1 fusion.73
  18.0 1.8 %collective-permute-start.1 = (f32[8,1,1,160]{3,2,1,0:T(1,128)S(1)}, f32[8,1,1,160]{3,2,1,0:T(1,128)S(1)}, u32[]{:S(2)}, u32[]{:S(2)}) collective-permute-start(f32[8,1,1,160]{3,2,1,0:T(1,128)S(1)} %get-tuple-element.127), channel_id=1, source_target_pairs={{0,4},{4,8},{8,12},{12,16},{16,20},{20,24},{24,28},{1,5},{5,9},{9,... | collective-permute-start | bytes 15368 | tf_op jit(solution)/shard_map/ppermute | solution.py:31
  19.9 1.3 %collective-permute-start = (f32[8,1,1,160]{3,2,1,0:T(1,128)S(1)}, f32[8,1,1,160]{3,2,1,0:T(1,128)S(1)}, u32[]{:S(2)}, u32[]{:S(2)}) collective-permute-start(f32[8,1,1,160]{3,2,1,0:T(1,128)S(1)} %get-tuple-element.127), channel_id=1, source_target_pairs={{4,0},{8,4},{12,8},{16,12},{20,16},{24,20},{28,24},{5,1},{9,5},{13... | collective-permute-start | bytes 15368 | tf_op jit(solution)/shard_map/ppermute | solution.py:32
  21.2 9.3 %all-gather.1 = f32[4,1,160]{2,1,0:T(1,128)S(1)} all-gather(f32[1,1,160]{2,1,0:T(1,128)S(1)} %bitcast.96), channel_id=2, replica_groups=mesh['wave'=8,'lev'=4] {'lev'}, dimensions={0}, use_global_device_ids=true | all-gather | bytes 3200 | tf_op jit(solution)/shard_map/all_gather | solution.py:13
  30.4 0.1 while.14
  30.5 0.0 collective-permute-done.2
  30.6 0.0 collective-permute-done.3
  30.6 0.0 collective-permute-done.1
  30.6 0.0 collective-permute-done
  30.6 0.1 fusion.40
  30.7 0.5 %fusion.13 = f32[8,80]{1,0:T(8,128)S(1)} fusion(s32[80]{0:T(128)S(1)} %copy-done.3, f32[8,1,1,160]{3,2,1,0:T(1,128)S(1)} %fusion.40), kind=kOutput, calls=%fused_computation.18 | convolution fusion | flops 1344000 | bytes 8000 | tf_op jit(solution)/shard_map/dot_general | solution.py:71
  31.2 0.6 %multiply_bitcast_fusion.1 = (f32[8,1,1,1,80]{4,0,3,2,1:T(8,128)S(1)}, f32[8,1,1,1,80]{4,0,3,2,1:T(8,128)S(1)}) fusion(f32[8,80]{1,0:T(8,128)S(1)} %fusion.13, s32[80]{0:T(128)S(1)} %copy-done.3, f32[8,1,1,160]{3,2,1,0:T(1,128)S(1)} %fusion.40), kind=kOutput, calls=%fused_computation.59 | convolution fusion | flops 1347840 | bytes 13120 | tf_op jit(solution)/shard_map/dot_general | solution.py:71
  31.8 0.1 copy.48
  32.0 0.5 %broadcast.613 = f32[]{:T(128)} broadcast(f32[]{:T(128)} %constant.216), dimensions={} | broadcast | bytes 8
  32.5 0.9 %reduce = f32[80,2,8]{2,1,0:T(2,128)S(1)} reduce(f32[80,2,1,1,8]{4,3,2,1,0:T(1,128)S(1)} %bitcast.92, f32[]{:T(128)} %broadcast.613), dimensions={2,3}, to_apply=%bitcast.79.reduce_sub_computation | reduce | bytes 10244
  33.4 0.1 reshape.695
  33.5 11.0 %all_to_all.21 = f32[8,1,160]{2,1,0:T(1,128)S(1)} all-to-all(f32[8,1,160]{2,1,0:T(1,128)S(1)} %reshape.695), channel_id=1, replica_groups=mesh['wave'=8,'lev'=4] {'wave'}, dimensions={0} | all-to-all | bytes 10240 | tf_op jit(solution)/shard_map/all_to_all | solution.py:180
  44.5 0.7 %reduce.1 = f32[8,160]{1,0:T(8,128)S(1)} reduce(f32[8,1,160]{2,1,0:T(1,128)S(1)} %all_to_all.21, f32[]{:T(128)} %broadcast.613), dimensions={1}, to_apply=%all_to_all.8.reduce_sub_computation | reduce | bytes 10244 | tf_op jit(solution)/shard_map/all_to_all | solution.py:180
  45.2 0.2 reshape.696
  45.4 0.3 fusion.1
  45.7 0.7 %copy.51 = f32[8,2,1,10,80]{4,2,3,1,0:T(1,128)} copy(f32[8,2,1,10,80]{4,0,1,3,2:T(8,128)S(1)} %fusion.1) | data formatting | bytes 102400 | tf_op jit(solution)/shard_map/jit(_where)/select_n | solution.py:184
  (26 shorter events, 0.2 us)
Async XLA Ops:
  0.0 2.6 %copy-start = (f32[10,8,80]{2,1,0:T(8,128)S(1)}, f32[10,8,80]{2,1,0:T(8,128)}, u32[]{:S(2)}) copy-start(f32[10,8,80]{2,1,0:T(8,128)} %param.10) | copy-start | bytes 76804
  0.1 0.7 %copy-start.3 = (s32[80]{0:T(128)S(1)}, s32[80]{0:T(128)}, u32[]{:S(2)}) copy-start(s32[80]{0:T(128)} %param.11) | copy-start | bytes 964
  1.1 0.7 %slice-start = ((f32[4,1,10,80]{3,1,2,0:T(1,128)}), f32[2,1,10,80]{3,1,2,0:T(1,128)S(1)}, s32[]{:S(2)}) async-start(f32[4,1,10,80]{3,1,2,0:T(1,128)} %param.9), calls=%async_computation.2 | async-start | bytes 20480 | tf_op jit(solution)/shard_map/slice | solution.py:59
  1.1 0.8 %copy-start.1 = (f32[4,1,10,80]{3,1,2,0:T(1,128)S(1)}, f32[4,1,10,80]{3,1,2,0:T(1,128)}, u32[]{:S(2)}) copy-start(f32[4,1,10,80]{3,1,2,0:T(1,128)} %param.9) | copy-start | bytes 38404
  3.5 5.3 %copy-start.2 = (f32[8,1,1,160]{3,2,1,0:T(1,128)S(1)}, f32[8,1,1,160]{3,2,1,0:T(1,128)}, u32[]{:S(2)}) copy-start(f32[8,1,1,160]{3,2,1,0:T(1,128)} %param.15) | copy-start | bytes 15364
  3.5 13.1 %all-to-all-start = ((f32[3,2,1,8,10]{4,1,0,2,3:T(2,128)}), f32[3,2,1,8,10]{4,1,0,2,3:T(2,128)S(1)}, u32[]{:S(2)}, u32[]{:S(2)}) async-start(f32[3,2,1,8,10]{4,1,0,2,3:T(2,128)} %copy.45), calls=%async_computation | async-start | bytes 49152 | tf_op jit(solution)/shard_map/all_to_all | solution.py:142
  8.8 21.7 %collective-permute-start.2 = (f32[8,1,1,160]{3,2,1,0:T(1,128)S(1)}, f32[8,1,1,160]{3,2,1,0:T(1,128)S(1)}, u32[]{:S(2)}, u32[]{:S(2)}) collective-permute-start(f32[8,1,1,160]{3,2,1,0:T(1,128)S(1)} %copy-done.2), channel_id=1, source_target_pairs={{1,0},{2,1},{3,2},{5,4},{6,5},{7,6},{9,8},{10,9},{11,10},{13,12},{... | collective-permute-start | bytes 15368 | tf_op jit(solution)/shard_map/ppermute | solution.py:32
  10.1 20.4 %collective-permute-start.3 = (f32[8,1,1,160]{3,2,1,0:T(1,128)S(1)}, f32[8,1,1,160]{3,2,1,0:T(1,128)S(1)}, u32[]{:S(2)}, u32[]{:S(2)}) collective-permute-start(f32[8,1,1,160]{3,2,1,0:T(1,128)S(1)} %copy-done.2), channel_id=1, source_target_pairs={{0,1},{1,2},{2,3},{4,5},{5,6},{6,7},{8,9},{9,10},{10,11},{12,13},{... | collective-permute-start | bytes 15368 | tf_op jit(solution)/shard_map/ppermute | solution.py:31
  18.0 12.5 %collective-permute-start.1 = (f32[8,1,1,160]{3,2,1,0:T(1,128)S(1)}, f32[8,1,1,160]{3,2,1,0:T(1,128)S(1)}, u32[]{:S(2)}, u32[]{:S(2)}) collective-permute-start(f32[8,1,1,160]{3,2,1,0:T(1,128)S(1)} %get-tuple-element.127), channel_id=1, source_target_pairs={{0,4},{4,8},{8,12},{12,16},{16,20},{20,24},{24,28},{1,5},{5,9},{9,... | collective-permute-start | bytes 15368 | tf_op jit(solution)/shard_map/ppermute | solution.py:31
  19.9 10.7 %collective-permute-start = (f32[8,1,1,160]{3,2,1,0:T(1,128)S(1)}, f32[8,1,1,160]{3,2,1,0:T(1,128)S(1)}, u32[]{:S(2)}, u32[]{:S(2)}) collective-permute-start(f32[8,1,1,160]{3,2,1,0:T(1,128)S(1)} %get-tuple-element.127), channel_id=1, source_target_pairs={{4,0},{8,4},{12,8},{16,12},{20,16},{24,20},{28,24},{5,1},{9,5},{13... | collective-permute-start | bytes 15368 | tf_op jit(solution)/shard_map/ppermute | solution.py:32
where the time goes:
time: 46.9 us; the launch traced here: 46.4 us
  blocking collectives  20.3 us (43%)
  starting transfers between devices  14.3 us (30%)
  local copies, waits for them, and re-layouts  4.59 us (10%)
  matrix products  2.69 us (6%)
  other arithmetic  2.31 us (5%)
  between operations  2.19 us (5%)
    all_to_all x1, blocking collectives, shards(): lax.all_to_all(spectra, 'wave', split_axis=4, concat_axis=3, tiled=True)  11 us
    all_gather x1, blocking collectives, prefix_2(): everything = lax.all_gather(shard, axis)  9.26 us
    ppermute x2, starting transfers between devices, with_halo(): before = lax.ppermute(last, axis, up)  6.38 us
    all_to_all x1, starting transfers between devices, shards(): lax.all_to_all(fourier, 'wave', split_axis=3, concat_axis=4, tiled=True)  5.31 us
    ppermute x2, starting transfers between devices, with_halo(): after = lax.ppermute(initial, axis, down)  2.58 us
    dot_general x4, matrix products, matmul(): jnp.dot(left, right, precision=lax.Precision.HIGHEST, preferred_element_t...  2.17 us
    unnamed x11, local copies, waits for them, and re-layouts  1.56 us
  transfers between devices with their start and end apart: 5, of which 0 were waited for; matrix products, arithmetic and copies ran while one was open for 3% of the time, Pallas kernels for 0%

commit v1 on v0

v1 whole, which is shorter than its diff:
```python
import functools
import math

import jax
import jax.numpy as jnp
from jax import lax
from jax.experimental import pallas as pl
from jax.experimental.pallas import tpu as pltpu
from jax.sharding import PartitionSpec as P

planet_radius = 20.0
MESH = pl.DeviceIdType.MESH
HIGHEST = lax.Precision.HIGHEST


def up_to(size, unit):
    return -(-size // unit) * unit


def each(count, body):
    if count <= 16:
        for i in range(count):
            body(i)
    else:

        def step(i, carry):
            body(i)
            return carry

        lax.fori_loop(0, count, step, 0)


def small_sin(x):
    y = x * x
    total = jnp.full_like(y, 1.0 / 6227020800.0)
    for c in (-1.0 / 39916800.0, 1.0 / 362880.0, -1.0 / 5040.0, 1.0 / 120.0, -1.0 / 6.0, 1.0):
        total = total * y + c
    return total * x


def kernel(
    n, levels, sizes,
    vd_ref, leg_ref, owner, sine_ref, weight_ref, thick_ref, q_ref,
    out_ref,
    vdp, table, legm, msg, recv1, qs, qn, lsend, recvl, send2, recv2,
    ss1, rs1, ssq, rsq, ssl, rsl, ss2, rs2,
):
    slots, lat, degrees, length, tracers = sizes
    wl = table.shape[1] // 2
    nd = vdp.shape[2]
    sp = vdp.shape[1]
    me = lax.axis_index("wave")
    lev = lax.axis_index("lev")

    qs[...] = q_ref[:, 0, 0, :]
    qn[...] = jnp.zeros_like(qn)
    recvl[...] = jnp.zeros_like(recvl)

    barrier = pltpu.get_barrier_semaphore()

    def greet_wave(d):
        pl.semaphore_signal(
            barrier, inc=1, device_id={"wave": lax.rem(me + d + 1, n)}, device_id_type=MESH
        )

    def greet_lev(d):
        pl.semaphore_signal(
            barrier, inc=1, device_id={"lev": lax.rem(lev + d + 1, levels)}, device_id_type=MESH
        )

    each(n - 1, greet_wave)
    each(levels - 1, greet_lev)

    vdp[...] = jnp.zeros_like(vdp)
    for f in range(4):
        vdp[f, :slots, :degrees] = vd_ref[f, 0]
    orders = [owner[me * slots + s].astype(jnp.float32) for s in range(slots)]
    sub = lax.broadcasted_iota(jnp.int32, (sp, nd), 0)
    degree = lax.broadcasted_iota(jnp.int32, (sp, nd), 1).astype(jnp.float32)
    order = jnp.zeros((sp, nd), jnp.float32)
    for s in range(slots):
        order = jnp.where(sub == s, orders[s], order)

    def coupling_at(d):
        ratio = jnp.maximum(d * d - order * order, 0.0) / jnp.maximum(4.0 * d * d - 1.0, 1.0)
        return jnp.where((d > order) & (d < degrees), jnp.sqrt(ratio), 0.0)

    lower_factor = -(degree - 1.0) * coupling_at(degree)
    upper_factor = (degree + 2.0) * coupling_at(degree + 1.0)
    inverse = jnp.where(
        degree > 0, -planet_radius * planet_radius / jnp.maximum(degree * (degree + 1.0), 1.0), 0.0
    )

    def derivative(field):
        return lower_factor * pltpu.roll(field, 1, 1) + upper_factor * pltpu.roll(field, nd - 1, 1)

    stream_real = inverse * vdp[0]
    stream_imag = inverse * vdp[1]
    potential_real = inverse * vdp[2]
    potential_imag = inverse * vdp[3]
    scale = 1.0 / planet_radius
    valid = degree >= order
    coefficients = [
        jnp.where(valid, c, 0.0)
        for c in (
            (-order * potential_imag - derivative(stream_real)) * scale,
            (order * potential_real - derivative(stream_imag)) * scale,
            (-order * stream_imag + derivative(potential_real)) * scale,
            (order * stream_real + derivative(potential_imag)) * scale,
            vdp[2],
            vdp[3],
        )
    ]

    lane = lax.broadcasted_iota(jnp.int32, (lat, wl), 1)
    fourier = [jnp.zeros((lat, wl), jnp.float32) for _ in range(6)]
    for s in range(slots):
        p_s = leg_ref[s]
        here = lane == s * n + me
        for f in range(6):
            total = jnp.sum(p_s * coefficients[f][s : s + 1, :degrees], axis=1, keepdims=True)
            fourier[f] = jnp.where(here, total, fourier[f])
    row = lax.broadcasted_iota(jnp.int32, (lat, wl), 0)

    def row_before(x):
        return jnp.where(row == 0, 0.0, pltpu.roll(x, 1, 0))

    def row_after(x):
        return jnp.where(row == lat - 1, 0.0, pltpu.roll(x, lat - 1, 0))

    for part in range(2):
        east, north, div = fourier[part], fourier[2 + part], fourier[4 + part]
        for t, value in enumerate((east, row_before(north), row_after(north), div)):
            msg[:, 4 * part + t, :] = value

    pl.semaphore_wait(barrier, n + levels - 2)

    def wave_copy(source, target, send, recv, d, buffer_at, out_at):
        return pltpu.make_async_remote_copy(
            src_ref=source.at[buffer_at],
            dst_ref=target.at[out_at],
            send_sem=send.at[d],
            recv_sem=recv.at[d],
            device_id={"wave": lax.rem(me + d + 1, n)},
            device_id_type=MESH,
        )

    def first(d):
        return wave_copy(msg, recv1, ss1, rs1, d, lax.rem(me + d + 1, n), me)

    each(n - 1, lambda d: first(d).start())

    halos = (
        ("wave", me, n, 1, 0),
        ("wave", me, n, -1, 1),
        ("lev", lev, levels, 1, 2),
        ("lev", lev, levels, -1, 3),
    )

    def halo_copy(axis, place, step, k):
        return pltpu.make_async_remote_copy(
            src_ref=qs,
            dst_ref=qn.at[k],
            send_sem=ssq.at[k],
            recv_sem=rsq.at[k],
            device_id={axis: place + step},
            device_id_type=MESH,
        )

    def sends(place, count, step):
        return place < count - 1 if step > 0 else place > 0

    for axis, place, count, step, k in halos:

        @pl.when(sends(place, count, step))
        def _():
            halo_copy(axis, place, step, k).start()

    lane1 = lax.broadcasted_iota(jnp.int32, (1, wl), 1)

    def put(l, held):
        number = owner[lax.rem(l, n) * slots + l // n].astype(jnp.float32)
        return jnp.where(lane1 == l, number, held)

    numbers = jnp.zeros((1, wl), jnp.float32)
    if slots * n <= 128:
        for l in range(slots * n):
            numbers = put(l, numbers)
    else:
        numbers = lax.fori_loop(0, slots * n, put, numbers)
    filled = lane1 < slots * n
    block = 32 if length % 32 == 0 else 8 if length % 8 == 0 else length

    def table_block(b):
        start = b * block
        if not isinstance(b, int):
            start = pl.multiple_of(start, block)
        lon = lax.broadcasted_iota(jnp.int32, (block, wl), 0).astype(jnp.float32)
        if isinstance(b, int):
            lon = lon + float(start)
        else:
            lon = lon + start.astype(jnp.float32)
        product = numbers * lon
        turn = product - length * jnp.floor(product * (1.0 / length))
        turn = jnp.where(turn < 0, turn + length, turn)
        turn = jnp.where(turn >= length, turn - length, turn)
        turn = jnp.where(turn > length / 2, turn - length, turn)
        size = jnp.abs(turn)
        unit = 2.0 * math.pi / length
        cosine = small_sin((length / 4 - size) * unit)
        sine = small_sin(jnp.minimum(size, length / 2 - size) * unit)
        minus_sine = jnp.where(turn > 0, -sine, sine)
        table[pl.ds(start, block), :wl] = jnp.where(filled, cosine, 0.0)
        table[pl.ds(start, block), wl:] = jnp.where(filled, minus_sine, 0.0)

    each(length // block, table_block)
    degree_row = lax.broadcasted_iota(jnp.int32, (lat, degrees), 1).astype(jnp.float32)
    for s in range(slots):
        legm[pl.ds(s * lat, lat), :] = jnp.where(degree_row >= orders[s], leg_ref[s], 0.0)

    recv1[me] = msg[me]

    def first_wait(d):
        source = lax.rem(me - d - 1 + n, n)
        pltpu.make_async_remote_copy(
            src_ref=msg.at[0],
            dst_ref=recv1.at[source],
            send_sem=ss1.at[d],
            recv_sem=rs1.at[d],
            device_id={"wave": source},
            device_id_type=MESH,
        ).wait_recv()

    each(n - 1, first_wait)
    got = jnp.sum(recv1[...], axis=0)
    thick = jnp.full((1, 1), thick_ref[0], jnp.float32)

    lsend[...] = got * thick

    def level_copy(d):
        return pltpu.make_async_remote_copy(
            src_ref=lsend,
            dst_ref=recvl.at[lev],
            send_sem=ssl.at[d],
            recv_sem=rsl.at[d],
            device_id={"lev": lev + d + 1},
            device_id_type=MESH,
        )

    def level_start(d):
        @pl.when(lev + d + 1 < levels)
        def _():
            level_copy(d).start()

    each(levels - 1, level_start)

    def to_grid(left):
        return lax.dot_general(
            left, table[...], (((1,), (1,)), ((), ())),
            precision=HIGHEST, preferred_element_type=jnp.float32,
        )

    grid = to_grid(jnp.concatenate([got[0:4], got[4:8]], axis=1))
    q = qs[...]
    lon_step = 2.0 * math.pi / length
    lat_step = math.pi / (slots * n)
    flux = grid[0:1] * q
    ahead = jnp.concatenate([flux[:, 1:], flux[:, :1]], axis=1)
    behind = jnp.concatenate([flux[:, -1:], flux[:, :-1]], axis=1)
    zonal = (ahead - behind) * (1.0 / (2.0 * lon_step))

    for axis, place, count, step, k in halos:

        @pl.when(sends(place, count, -step))
        def _():
            halo_copy(axis, place, -step, k).wait_recv()

    merid = (grid[2:3] * qn[1] - grid[1:2] * qn[0]) * (1.0 / (2.0 * lat_step))
    sine = jnp.full((1, 1), sine_ref[0], jnp.float32)
    base = (zonal + merid) / (1.0 - sine * sine)
    layer = grid[3:4] * thick
    above = qn[2]
    below = qn[3]

    def level_wait(d):
        @pl.when(lev - d - 1 >= 0)
        def _():
            pltpu.make_async_remote_copy(
                src_ref=lsend,
                dst_ref=recvl.at[lev - d - 1],
                send_sem=ssl.at[d],
                recv_sem=rsl.at[d],
                device_id={"lev": lev - d - 1},
                device_id_type=MESH,
            ).wait_recv()

    each(levels - 1, level_wait)
    higher = jnp.sum(recvl[...], axis=0)
    prefix = to_grid(jnp.concatenate([higher[3:4], higher[7:8]], axis=1))
    omega_bottom = -(prefix + layer)
    omega_top = -prefix
    vertical = (omega_bottom * (q + below) * 0.5 - omega_top * (above + q) * 0.5) / thick
    weight = jnp.full((1, 1), weight_ref[0], jnp.float32)
    tendency = -weight * (base + vertical)

    spectra = lax.dot_general(
        tendency, table[...], (((1,), (0,)), ((), ())),
        precision=HIGHEST, preferred_element_type=jnp.float32,
    ) * (2.0 / length)
    spectra = jnp.concatenate([spectra[:, :wl], spectra[:, wl:]], axis=0)

    def second(d):
        return wave_copy(send2, recv2, ss2, rs2, d, d, me)

    def second_start(d):
        shift = lax.rem(wl + me - lax.rem(me + d + 1, n), wl)
        send2[d] = pltpu.roll(spectra, shift, 1)
        second(d).start()

    each(n - 1, second_start)
    recv2[me] = spectra

    def second_wait(d):
        source = lax.rem(me - d - 1 + n, n)
        pltpu.make_async_remote_copy(
            src_ref=send2.at[d],
            dst_ref=recv2.at[source],
            send_sem=ss2.at[d],
            recv_sem=rs2.at[d],
            device_id={"wave": source},
            device_id_type=MESH,
        ).wait_recv()

    each(n - 1, second_wait)
    lane2 = lax.broadcasted_iota(jnp.int32, (2 * tracers, wl), 1)
    row_of = lax.rem(lane2, n)
    gathered = jnp.zeros((2 * tracers, wl), jnp.float32)
    if n <= 16:
        for i in range(n):
            gathered = jnp.where(row_of == i, recv2[i], gathered)
    else:
        gathered = lax.fori_loop(
            0, n, lambda i, g: jnp.where(row_of == i, recv2[i], g), gathered
        )
    lane3 = lax.broadcasted_iota(jnp.int32, (sp, wl), 1)
    sub3 = lax.broadcasted_iota(jnp.int32, (sp, wl), 0)
    own = (lane3 >= sub3 * n) & (lane3 < sub3 * n + n)
    blocks = []
    for c in range(tracers):
        for r in range(2):
            i = r * tracers + c
            blocks.append(jnp.where(own, gathered[i : i + 1], 0.0))
    left = jnp.concatenate(blocks, axis=0)[:, : slots * n]
    result = jnp.dot(left, legm[...], precision=HIGHEST, preferred_element_type=jnp.float32)
    for c in range(tracers):
        for r in range(2):
            at = (c * 2 + r) * sp
            out_ref[c, r, 0] = result[at : at + slots]

    each(n - 1, lambda d: first(d).wait_send())
    each(n - 1, lambda d: second(d).wait_send())
    for axis, place, count, step, k in halos:

        @pl.when(sends(place, count, step))
        def _():
            halo_copy(axis, place, step, k).wait_send()

    def level_sent(d):
        @pl.when(lev + d + 1 < levels)
        def _():
            level_copy(d).wait_send()

    each(levels - 1, level_sent)


def shards(vort_div, legendre, owner_map, lat_sine, quad_weight, thickness, tracers):
    slots, lat, degrees = legendre.shape
    count, own_levels, own_rows, length = tracers.shape
    n, levels = lax.axis_size("wave"), lax.axis_size("lev")
    assert own_levels == 1 and own_rows == 1 and lat == n
    wl = up_to(slots * n, 128)
    nd = up_to(degrees, 128)
    sp = up_to(slots, 8)
    f32 = jnp.float32
    shapes = [
        ((4, sp, nd), f32),
        ((length, 2 * wl), f32),
        ((slots * lat, degrees), f32),
        ((n, 8, wl), f32),
        ((n, 8, wl), f32),
        ((count, length), f32),
        ((4, count, length), f32),
        ((8, wl), f32),
        ((levels, 8, wl), f32),
        ((n - 1, 2 * count, wl), f32),
        ((n, 2 * count, wl), f32),
    ]
    dma = pltpu.SemaphoreType.DMA
    vmem = pl.BlockSpec(memory_space=pltpu.VMEM)
    smem = pl.BlockSpec(memory_space=pltpu.SMEM)
    scratch_bytes = sum(4 * math.prod(shape) for shape, _ in shapes)
    return pl.pallas_call(
        functools.partial(kernel, n, levels, (slots, lat, degrees, length, count)),
        out_shape=jax.ShapeDtypeStruct((count, 2, 1, slots, degrees), f32),
        in_specs=[vmem, vmem, smem, smem, smem, smem, vmem],
        out_specs=vmem,
        scratch_shapes=[pltpu.VMEM(shape, kind) for shape, kind in shapes]
        + [dma((n - 1,)), dma((n - 1,)), dma((4,)), dma((4,))]
        + [dma((levels - 1,)), dma((levels - 1,)), dma((n - 1,)), dma((n - 1,))],
        compiler_params=pltpu.CompilerParams(
            collective_id=0,
            has_side_effects=True,
            vmem_limit_bytes=min(2 * scratch_bytes + (12 << 20), 60 << 20),
        ),
    )(vort_div, legendre, owner_map, lat_sine, quad_weight, thickness, tracers)


def solution(mesh):
    placed = (
        P(None, "lev", "wave", None),
        P("wave", None, None),
        P(),
        P("wave"),
        P("wave"),
        P("lev"),
        P(None, "lev", "wave", None),
    )
    return jax.shard_map(
        shards,
        mesh=mesh,
        in_specs=placed,
        out_specs=P(None, None, "lev", "wave", None),
        check_vma=False,
    )
```

time: 46.9 us -> 18.1 us (0.39)
  the two profiles are of different devices: /device:TPU:0 before, /device:TPU:9 now
where the time goes in v1:
time: 18.1 us; the launch traced here: 17.9 us
  Pallas kernels  14.4 us (80%)
  between operations  1.98 us (11%)
  local copies, waits for them, and re-layouts  1.47 us (8%)
    pallas_call x1, Pallas kernels, shards(): pl.pallas_call(functools.partial(kernel, n, levels, (slots, lat, degrees,...  14.4 us
    unnamed x7, local copies, waits for them, and re-layouts  0.75 us
    pallas_call x1, local copies, waits for them, and re-layouts, shards(): pl.pallas_call(functools.partial(kernel, n, levels, (slots, lat, degrees,...  0.72 us

profile of v1, /device:TPU:9, one launch (start us, length us, event | category | flops | bytes accessed | tf_op | source)
XLA Modules:
  0.0 17.9 jit_solution(16901435822475929952)
XLA Ops:
  0.0 0.0 copy-start
  2.0 0.0 copy-start.1
  2.0 0.0 copy-start.2
  2.0 0.7 %copy.8.vd_ref = f32[4,1,10,80]{3,2,1,0:T(8,128)S(1)} copy(f32[4,1,10,80]{3,1,2,0:T(1,128)} %param.7) | data formatting | bytes 25600 | tf_op args[0]
  2.7 0.0 copy-done
  2.7 0.0 copy-done.1
  2.7 0.0 copy-done.2
  2.7 14.4 %shard_map.73 = f32[8,2,1,10,80]{4,3,2,1,0:T(8,128)S(1)} custom-call(f32[4,1,10,80]{3,2,1,0:T(8,128)S(1)} %copy.8.vd_ref, f32[10,8,80]{2,1,0:T(8,128)S(1)} %copy-done, s32[80]{0:T(128)S(1)} %copy-done.2, f32[1]{0:T(128)S(6)} %copy.10.sine_ref, f32[1]{0:T(128)S(6)} %copy.11.weight_ref, f32[1]{0:T(128)S(6)} %copy.12.thick_ref, f32[8,1,1,160]{3,2,1,0:T(1,128)S(1)} %copy-done.1), custom_call_target="tpu_custom_call" | custom-call | tf_op jit(solution)/shard_map/pallas_call | solution.py:402
  17.2 0.7 %copy.9 = f32[8,2,1,10,80]{4,2,3,1,0:T(1,128)} copy(f32[8,2,1,10,80]{4,3,2,1,0:T(8,128)S(1)} %shard_map.73) | data formatting | bytes 102400 | tf_op jit(solution)/shard_map/pallas_call | solution.py:402
Async XLA Ops:
  0.0 2.7 %copy-start = (f32[10,8,80]{2,1,0:T(8,128)S(1)}, f32[10,8,80]{2,1,0:T(8,128)}, u32[]{:S(2)}) copy-start(f32[10,8,80]{2,1,0:T(8,128)} %leg_ref.1) | copy-start | bytes 76804
  2.0 0.8 %copy-start.1 = (f32[8,1,1,160]{3,2,1,0:T(1,128)S(1)}, f32[8,1,1,160]{3,2,1,0:T(1,128)}, u32[]{:S(2)}) copy-start(f32[8,1,1,160]{3,2,1,0:T(1,128)} %q_ref.1) | copy-start | bytes 15364
  2.0 0.8 %copy-start.2 = (s32[80]{0:T(128)S(1)}, s32[80]{0:T(128)}, u32[]{:S(2)}) copy-start(s32[80]{0:T(128)} %owner.1) | copy-start | bytes 964

commit v2 on v1

--- a/solution.py
+++ b/solution.py
@@ -10,7 +10,6 @@
 
 planet_radius = 20.0
 MESH = pl.DeviceIdType.MESH
-HIGHEST = lax.Precision.HIGHEST
 
 
 def up_to(size, unit):
@@ -18,7 +17,7 @@
 
 
 def each(count, body):
-    if count <= 16:
+    if count <= 32:
         for i in range(count):
             body(i)
     else:
@@ -28,6 +27,22 @@
             return carry
 
         lax.fori_loop(0, count, step, 0)
+
+
+def halves(x):
+    high = x.astype(jnp.bfloat16).astype(jnp.float32)
+    return high, x - high
+
+
+def split_dot(left, right_high, right_low, dims):
+    rows = left.shape[0]
+    high, low = halves(left)
+    both = jnp.concatenate([high, low], axis=0).astype(jnp.bfloat16)
+    dot = functools.partial(
+        lax.dot_general, dimension_numbers=(dims, ((), ())), preferred_element_type=jnp.float32
+    )
+    first = dot(both, right_high)
+    return first[:rows] + first[rows:] + dot(high.astype(jnp.bfloat16), right_low)
 
 
 def small_sin(x):
@@ -40,46 +55,70 @@
 
 def kernel(
     n, levels, sizes,
-    vd_ref, leg_ref, owner, sine_ref, weight_ref, thick_ref, q_ref,
+    vd_in, leg_in, owner_in, sine_in, weight_in, thick_in, q_in,
     out_ref,
-    vdp, table, legm, msg, recv1, qs, qn, lsend, recvl, send2, recv2,
-    ss1, rs1, ssq, rsq, ssl, rsl, ss2, rs2,
+    vd_ref, leg_ref, owner_ref, sine_ref, weight_ref, thick_ref, q_ref,
+    vdp, thigh, tlow, lhigh, llow, msg, recv1, qs, qn, dmsg, recvd, send2, recv2,
+    ssi, ss1, rs1, ssq, rsq, ssd, rsd, ss2, rs2,
 ):
     slots, lat, degrees, length, tracers = sizes
-    wl = table.shape[1] // 2
+    wl = thigh.shape[1] // 2
     nd = vdp.shape[2]
     sp = vdp.shape[1]
     me = lax.axis_index("wave")
     lev = lax.axis_index("lev")
 
+    loads = [
+        pltpu.make_async_copy(source, target, ssi.at[i])
+        for i, (source, target) in enumerate(
+            (
+                (vd_in, vd_ref),
+                (owner_in, owner_ref),
+                (leg_in, leg_ref),
+                (q_in, q_ref),
+                (thick_in, thick_ref),
+                (sine_in, sine_ref),
+                (weight_in, weight_ref),
+            )
+        )
+    ]
+    for load in loads:
+        load.start()
+    qn[...] = jnp.zeros_like(qn)
+    recvd[...] = jnp.zeros_like(recvd)
+
+    barrier = pltpu.get_barrier_semaphore()
+
+    def greet(d):
+        pl.semaphore_signal(
+            barrier,
+            inc=1,
+            device_id={
+                "wave": lax.rem(me + (d + 1) % n, n),
+                "lev": lax.rem(lev + (d + 1) // n, levels),
+            },
+            device_id_type=MESH,
+        )
+
+    each(n * levels - 1, greet)
+
+    vdp[...] = jnp.zeros_like(vdp)
+    for load in loads:
+        load.wait()
+    for f in range(4):
+        vdp[f, :slots, :degrees] = vd_ref[f, :, 0]
     qs[...] = q_ref[:, 0, 0, :]
-    qn[...] = jnp.zeros_like(qn)
-    recvl[...] = jnp.zeros_like(recvl)
-
-    barrier = pltpu.get_barrier_semaphore()
-
-    def greet_wave(d):
-        pl.semaphore_signal(
-            barrier, inc=1, device_id={"wave": lax.rem(me + d + 1, n)}, device_id_type=MESH
-        )
-
-    def greet_lev(d):
-        pl.semaphore_signal(
-            barrier, inc=1, device_id={"lev": lax.rem(lev + d + 1, levels)}, device_id_type=MESH
-        )
-
-    each(n - 1, greet_wave)
-    each(levels - 1, greet_lev)
-
-    vdp[...] = jnp.zeros_like(vdp)
-    for f in range(4):
-        vdp[f, :slots, :degrees] = vd_ref[f, 0]
-    orders = [owner[me * slots + s].astype(jnp.float32) for s in range(slots)]
+    owner = owner_ref[...].astype(jnp.float32)
+    total_slots = owner.shape[1]
+    place_at = lax.broadcasted_iota(jnp.int32, (sp, total_slots), 1)
+    slot_at = lax.broadcasted_iota(jnp.int32, (sp, total_slots), 0)
+    own_order = jnp.sum(
+        jnp.where(place_at == me * slots + slot_at, owner, 0.0), axis=1, keepdims=True
+    )
+    thick = thick_ref[...].reshape(1, 1)
     sub = lax.broadcasted_iota(jnp.int32, (sp, nd), 0)
     degree = lax.broadcasted_iota(jnp.int32, (sp, nd), 1).astype(jnp.float32)
-    order = jnp.zeros((sp, nd), jnp.float32)
-    for s in range(slots):
-        order = jnp.where(sub == s, orders[s], order)
+    order = jnp.where(sub < slots, own_order, 0.0)
 
     def coupling_at(d):
         ratio = jnp.maximum(d * d - order * order, 0.0) / jnp.maximum(4.0 * d * d - 1.0, 1.0)
@@ -132,8 +171,9 @@
         east, north, div = fourier[part], fourier[2 + part], fourier[4 + part]
         for t, value in enumerate((east, row_before(north), row_after(north), div)):
             msg[:, 4 * part + t, :] = value
-
-    pl.semaphore_wait(barrier, n + levels - 2)
+        dmsg[:, part, :] = div * thick
+
+    pl.semaphore_wait(barrier, n * levels - 1)
 
     def wave_copy(source, target, send, recv, d, buffer_at, out_at):
         return pltpu.make_async_remote_copy(
@@ -150,6 +190,22 @@
 
     each(n - 1, lambda d: first(d).start())
 
+    def mass(k):
+        up, to = k // n, k % n
+
+        @pl.when(lev + up + 1 < levels)
+        def _():
+            pltpu.make_async_remote_copy(
+                src_ref=dmsg.at[to],
+                dst_ref=recvd.at[lev, me],
+                send_sem=ssd.at[up],
+                recv_sem=rsd.at[up],
+                device_id={"wave": to, "lev": lev + up + 1},
+                device_id_type=MESH,
+            ).start()
+
+    each((levels - 1) * n, mass)
+
     halos = (
         ("wave", me, n, 1, 0),
         ("wave", me, n, -1, 1),
@@ -177,17 +233,16 @@
             halo_copy(axis, place, step, k).start()
 
     lane1 = lax.broadcasted_iota(jnp.int32, (1, wl), 1)
-
-    def put(l, held):
-        number = owner[lax.rem(l, n) * slots + l // n].astype(jnp.float32)
-        return jnp.where(lane1 == l, number, held)
-
-    numbers = jnp.zeros((1, wl), jnp.float32)
-    if slots * n <= 128:
-        for l in range(slots * n):
-            numbers = put(l, numbers)
-    else:
-        numbers = lax.fori_loop(0, slots * n, put, numbers)
+    target = lax.broadcasted_iota(jnp.int32, (wl, total_slots), 0)
+    source_at = lax.broadcasted_iota(jnp.int32, (wl, total_slots), 1)
+    column = jnp.sum(
+        jnp.where(source_at == lax.rem(target, n) * slots + target // n, owner, 0.0),
+        axis=1,
+        keepdims=True,
+    )
+    square = (wl, wl)
+    diagonal = lax.broadcasted_iota(jnp.int32, square, 0) == lax.broadcasted_iota(jnp.int32, square, 1)
+    numbers = jnp.sum(jnp.where(diagonal, column, 0.0), axis=0, keepdims=True)
     filled = lane1 < slots * n
     block = 32 if length % 32 == 0 else 8 if length % 8 == 0 else length
 
@@ -210,13 +265,20 @@
         cosine = small_sin((length / 4 - size) * unit)
         sine = small_sin(jnp.minimum(size, length / 2 - size) * unit)
         minus_sine = jnp.where(turn > 0, -sine, sine)
-        table[pl.ds(start, block), :wl] = jnp.where(filled, cosine, 0.0)
-        table[pl.ds(start, block), wl:] = jnp.where(filled, minus_sine, 0.0)
+        for part, value in enumerate((cosine, minus_sine)):
+            high, low = halves(jnp.where(filled, value, 0.0))
+            at = (pl.ds(start, block), pl.ds(part * wl, wl))
+            thigh[at] = high.astype(jnp.bfloat16)
+            tlow[at] = low.astype(jnp.bfloat16)
 
     each(length // block, table_block)
     degree_row = lax.broadcasted_iota(jnp.int32, (lat, degrees), 1).astype(jnp.float32)
-    for s in range(slots):
-        legm[pl.ds(s * lat, lat), :] = jnp.where(degree_row >= orders[s], leg_ref[s], 0.0)
+    masked = jnp.concatenate(
+        [jnp.where(degree_row >= own_order[s : s + 1], leg_ref[s], 0.0) for s in range(slots)], axis=0
+    )
+    high, low = halves(masked)
+    lhigh[...] = high.astype(jnp.bfloat16)
+    llow[...] = low.astype(jnp.bfloat16)
 
     recv1[me] = msg[me]
 
@@ -233,34 +295,29 @@
 
     each(n - 1, first_wait)
     got = jnp.sum(recv1[...], axis=0)
-    thick = jnp.full((1, 1), thick_ref[0], jnp.float32)
-
-    lsend[...] = got * thick
-
-    def level_copy(d):
-        return pltpu.make_async_remote_copy(
-            src_ref=lsend,
-            dst_ref=recvl.at[lev],
-            send_sem=ssl.at[d],
-            recv_sem=rsl.at[d],
-            device_id={"lev": lev + d + 1},
-            device_id_type=MESH,
-        )
-
-    def level_start(d):
-        @pl.when(lev + d + 1 < levels)
-        def _():
-            level_copy(d).start()
-
-    each(levels - 1, level_start)
-
-    def to_grid(left):
-        return lax.dot_general(
-            left, table[...], (((1,), (1,)), ((), ())),
-            precision=HIGHEST, preferred_element_type=jnp.float32,
-        )
-
-    grid = to_grid(jnp.concatenate([got[0:4], got[4:8]], axis=1))
+
+    def mass_wait(d):
+        @pl.when(lev - d - 1 >= 0)
+        def _():
+            pltpu.make_async_remote_copy(
+                src_ref=dmsg,
+                dst_ref=recvd.at[lev - d - 1],
+                send_sem=ssd.at[d],
+                recv_sem=rsd.at[d],
+                device_id={"lev": lev - d - 1},
+                device_id_type=MESH,
+            ).wait_recv()
+
+    each(levels - 1, mass_wait)
+    higher = jnp.sum(jnp.sum(recvd[...], axis=0), axis=0)
+    left = jnp.concatenate(
+        [
+            jnp.concatenate([got[0:4], higher[0:1], jnp.zeros((3, wl), jnp.float32)], axis=0),
+            jnp.concatenate([got[4:8], higher[1:2], jnp.zeros((3, wl), jnp.float32)], axis=0),
+        ],
+        axis=1,
+    )
+    grid = split_dot(left, thigh[...], tlow[...], ((1,), (1,)))
     q = qs[...]
     lon_step = 2.0 * math.pi / length
     lat_step = math.pi / (slots * n)
@@ -276,37 +333,19 @@
             halo_copy(axis, place, -step, k).wait_recv()
 
     merid = (grid[2:3] * qn[1] - grid[1:2] * qn[0]) * (1.0 / (2.0 * lat_step))
-    sine = jnp.full((1, 1), sine_ref[0], jnp.float32)
+    sine = sine_ref[...].reshape(1, 1)
     base = (zonal + merid) / (1.0 - sine * sine)
     layer = grid[3:4] * thick
     above = qn[2]
     below = qn[3]
 
-    def level_wait(d):
-        @pl.when(lev - d - 1 >= 0)
-        def _():
-            pltpu.make_async_remote_copy(
-                src_ref=lsend,
-                dst_ref=recvl.at[lev - d - 1],
-                send_sem=ssl.at[d],
-                recv_sem=rsl.at[d],
-                device_id={"lev": lev - d - 1},
-                device_id_type=MESH,
-            ).wait_recv()
-
-    each(levels - 1, level_wait)
-    higher = jnp.sum(recvl[...], axis=0)
-    prefix = to_grid(jnp.concatenate([higher[3:4], higher[7:8]], axis=1))
+    prefix = grid[4:5]
     omega_bottom = -(prefix + layer)
     omega_top = -prefix
     vertical = (omega_bottom * (q + below) * 0.5 - omega_top * (above + q) * 0.5) / thick
-    weight = jnp.full((1, 1), weight_ref[0], jnp.float32)
-    tendency = -weight * (base + vertical)
-
-    spectra = lax.dot_general(
-        tendency, table[...], (((1,), (0,)), ((), ())),
-        precision=HIGHEST, preferred_element_type=jnp.float32,
-    ) * (2.0 / length)
+    tendency = -weight_ref[...].reshape(1, 1) * (base + vertical)
+
+    spectra = split_dot(tendency, thigh[...], tlow[...], ((1,), (0,))) * (2.0 / length)
     spectra = jnp.concatenate([spectra[:, :wl], spectra[:, wl:]], axis=0)
 
     def second(d):
@@ -351,11 +390,11 @@
             i = r * tracers + c
             blocks.append(jnp.where(own, gathered[i : i + 1], 0.0))
     left = jnp.concatenate(blocks, axis=0)[:, : slots * n]
-    result = jnp.dot(left, legm[...], precision=HIGHEST, preferred_element_type=jnp.float32)
+    result = split_dot(left, lhigh[...], llow[...], ((1,), (0,)))
     for c in range(tracers):
         for r in range(2):
             at = (c * 2 + r) * sp
-            out_ref[c, r, 0] = result[at : at + slots]
+            out_ref[c, r, :, 0, :] = result[at : at + slots]
 
     each(n - 1, lambda d: first(d).wait_send())
     each(n - 1, lambda d: second(d).wait_send())
@@ -365,12 +404,19 @@
         def _():
             halo_copy(axis, place, step, k).wait_send()
 
-    def level_sent(d):
+    def mass_sent(d):
         @pl.when(lev + d + 1 < levels)
         def _():
-            level_copy(d).wait_send()
-
-    each(levels - 1, level_sent)
+            pltpu.make_async_remote_copy(
+                src_ref=dmsg,
+                dst_ref=recvd.at[lev],
+                send_sem=ssd.at[d],
+                recv_sem=rsd.at[d],
+                device_id={"lev": lev + d + 1},
+                device_id_type=MESH,
+            ).wait_send()
+
+    each(levels - 1, mass_sent)
 
 
 def shards(vort_div, legendre, owner_map, lat_sine, quad_weight, thickness, tracers):
@@ -382,37 +428,48 @@
     nd = up_to(degrees, 128)
     sp = up_to(slots, 8)
     f32 = jnp.float32
-    shapes = [
+    bf16 = jnp.bfloat16
+    operands = (
+        jnp.transpose(vort_div, (0, 2, 1, 3)),
+        legendre,
+        owner_map.reshape(1, -1),
+        lat_sine,
+        quad_weight,
+        thickness,
+        tracers,
+    )
+    shapes = [(x.shape, x.dtype) for x in operands] + [
         ((4, sp, nd), f32),
-        ((length, 2 * wl), f32),
-        ((slots * lat, degrees), f32),
+        ((length, 2 * wl), bf16),
+        ((length, 2 * wl), bf16),
+        ((slots * lat, degrees), bf16),
+        ((slots * lat, degrees), bf16),
         ((n, 8, wl), f32),
         ((n, 8, wl), f32),
         ((count, length), f32),
         ((4, count, length), f32),
-        ((8, wl), f32),
-        ((levels, 8, wl), f32),
+        ((n, 2, wl), f32),
+        ((levels, n, 2, wl), f32),
         ((n - 1, 2 * count, wl), f32),
         ((n, 2 * count, wl), f32),
     ]
     dma = pltpu.SemaphoreType.DMA
-    vmem = pl.BlockSpec(memory_space=pltpu.VMEM)
-    smem = pl.BlockSpec(memory_space=pltpu.SMEM)
     scratch_bytes = sum(4 * math.prod(shape) for shape, _ in shapes)
-    return pl.pallas_call(
+    result = pl.pallas_call(
         functools.partial(kernel, n, levels, (slots, lat, degrees, length, count)),
-        out_shape=jax.ShapeDtypeStruct((count, 2, 1, slots, degrees), f32),
-        in_specs=[vmem, vmem, smem, smem, smem, smem, vmem],
-        out_specs=vmem,
+        out_shape=jax.ShapeDtypeStruct((count, 2, slots, 1, degrees), f32),
+        in_specs=[pl.BlockSpec(memory_space=pltpu.HBM)] * len(operands),
+        out_specs=pl.BlockSpec(memory_space=pltpu.VMEM),
         scratch_shapes=[pltpu.VMEM(shape, kind) for shape, kind in shapes]
-        + [dma((n - 1,)), dma((n - 1,)), dma((4,)), dma((4,))]
+        + [dma((len(operands),)), dma((n - 1,)), dma((n - 1,)), dma((4,)), dma((4,))]
         + [dma((levels - 1,)), dma((levels - 1,)), dma((n - 1,)), dma((n - 1,))],
         compiler_params=pltpu.CompilerParams(
             collective_id=0,
             has_side_effects=True,
-            vmem_limit_bytes=min(2 * scratch_bytes + (12 << 20), 60 << 20),
+            vmem_limit_bytes=63 << 20,
         ),
-    )(vort_div, legendre, owner_map, lat_sine, quad_weight, thickness, tracers)
+    )(*operands)
+    return jnp.transpose(result, (0, 1, 3, 2, 4))
 
 
 def solution(mesh):

time: 18.1 us -> 18.8 us (1.039)
  the two profiles are of different devices: /device:TPU:9 before, /device:TPU:0 now
where the time goes in v2:
time: 18.8 us; the launch traced here: 18.6 us
  Pallas kernels  15.1 us (80%)
  between operations  1.95 us (10%)
  local copies, waits for them, and re-layouts  1.53 us (8%)
    pallas_call x1, Pallas kernels, shards(): pl.pallas_call(functools.partial(kernel, n, levels, (slots, lat, degrees,...  15.1 us
    unnamed x1, local copies, waits for them, and re-layouts  1.53 us

profile of v2, /device:TPU:0, one launch (start us, length us, event | category | flops | bytes accessed | tf_op | source)
XLA Modules:
  0.0 18.6 jit_solution(1630311713267091850)
XLA Ops:
  1.9 15.1 %shard_map.73 = f32[8,2,10,1,80]{4,3,2,1,0:T(1,128)} custom-call(f32[4,10,1,80]{3,2,1,0:T(1,128)} %bitcast.4, f32[10,8,80]{2,1,0:T(8,128)} %leg_in.1, s32[1,80]{1,0:T(1,128)} %bitcast.5, f32[1]{0:T(128)S(6)} %copy.9.sine_in, f32[1]{0:T(128)S(6)} %copy.10.weight_in, f32[1]{0:T(128)S(6)} %copy.11.thick_in, f32[8,1,1,160]{3,2,1,0:T(1,128)} %q_in.1), custom_call_target="tpu_custom_call" | custom-call | tf_op jit(solution)/shard_map/pallas_call | solution.py:458
  17.1 1.5 %copy.12 = f32[8,2,1,10,80]{4,2,3,1,0:T(1,128)} copy(f32[8,2,1,10,80]{4,2,3,1,0:T(1,128)} %bitcast.3) | data formatting | bytes 102400

commit v3 on v2

--- a/solution.py
+++ b/solution.py
@@ -55,11 +55,10 @@
 
 def kernel(
     n, levels, sizes,
-    vd_in, leg_in, owner_in, sine_in, weight_in, thick_in, q_in,
+    vd_ref, leg_ref, owner_ref, sine_ref, weight_ref, thick_ref, q_ref,
     out_ref,
-    vd_ref, leg_ref, owner_ref, sine_ref, weight_ref, thick_ref, q_ref,
     vdp, thigh, tlow, lhigh, llow, msg, recv1, qs, qn, dmsg, recvd, send2, recv2,
-    ssi, ss1, rs1, ssq, rsq, ssd, rsd, ss2, rs2,
+    ss1, rs1, ssq, rsq, ssd, rsd, ss2, rs2,
 ):
     slots, lat, degrees, length, tracers = sizes
     wl = thigh.shape[1] // 2
@@ -68,22 +67,6 @@
     me = lax.axis_index("wave")
     lev = lax.axis_index("lev")
 
-    loads = [
-        pltpu.make_async_copy(source, target, ssi.at[i])
-        for i, (source, target) in enumerate(
-            (
-                (vd_in, vd_ref),
-                (owner_in, owner_ref),
-                (leg_in, leg_ref),
-                (q_in, q_ref),
-                (thick_in, thick_ref),
-                (sine_in, sine_ref),
-                (weight_in, weight_ref),
-            )
-        )
-    ]
-    for load in loads:
-        load.start()
     qn[...] = jnp.zeros_like(qn)
     recvd[...] = jnp.zeros_like(recvd)
 
@@ -103,8 +86,6 @@
     each(n * levels - 1, greet)
 
     vdp[...] = jnp.zeros_like(vdp)
-    for load in loads:
-        load.wait()
     for f in range(4):
         vdp[f, :slots, :degrees] = vd_ref[f, :, 0]
     qs[...] = q_ref[:, 0, 0, :]
@@ -438,7 +419,7 @@
         thickness,
         tracers,
     )
-    shapes = [(x.shape, x.dtype) for x in operands] + [
+    shapes = [
         ((4, sp, nd), f32),
         ((length, 2 * wl), bf16),
         ((length, 2 * wl), bf16),
@@ -458,15 +439,15 @@
     result = pl.pallas_call(
         functools.partial(kernel, n, levels, (slots, lat, degrees, length, count)),
         out_shape=jax.ShapeDtypeStruct((count, 2, slots, 1, degrees), f32),
-        in_specs=[pl.BlockSpec(memory_space=pltpu.HBM)] * len(operands),
+        in_specs=[pl.BlockSpec(memory_space=pltpu.VMEM)] * len(operands),
         out_specs=pl.BlockSpec(memory_space=pltpu.VMEM),
         scratch_shapes=[pltpu.VMEM(shape, kind) for shape, kind in shapes]
-        + [dma((len(operands),)), dma((n - 1,)), dma((n - 1,)), dma((4,)), dma((4,))]
+        + [dma((n - 1,)), dma((n - 1,)), dma((4,)), dma((4,))]
         + [dma((levels - 1,)), dma((levels - 1,)), dma((n - 1,)), dma((n - 1,))],
         compiler_params=pltpu.CompilerParams(
             collective_id=0,
             has_side_effects=True,
-            vmem_limit_bytes=63 << 20,
+            vmem_limit_bytes=min(2 * scratch_bytes + (8 << 20), 60 << 20),
         ),
     )(*operands)
     return jnp.transpose(result, (0, 1, 3, 2, 4))

time: 18.8 us -> 19.5 us (1.037)
  local copies, waits for them, and re-layouts: 1.53 us -> 2.78 us
  Pallas kernels: 15.1 us -> 14.4 us
    unnamed x1 -> x9, local copies, waits for them, and re-layouts: 1.53 us -> 2.78 us
    pallas_call x1, Pallas kernels: 15.1 us -> 14.4 us  [shards(): pl.pallas_call(functools.partial(kernel, n, levels, (slots, lat, degrees,...]
where the time goes in v3:
time: 19.5 us; the launch traced here: 19.2 us
  Pallas kernels  14.4 us (74%)
  local copies, waits for them, and re-layouts  2.78 us (14%)
  between operations  1.98 us (10%)
    pallas_call x1, Pallas kernels, shards(): pl.pallas_call(functools.partial(kernel, n, levels, (slots, lat, degrees,...  14.4 us
    unnamed x9, local copies, waits for them, and re-layouts  2.78 us

profile of v3, /device:TPU:0, one launch (start us, length us, event | category | flops | bytes accessed | tf_op | source)
XLA Modules:
  0.0 19.2 jit_solution(13048550314561743055)
XLA Ops:
  0.0 0.0 copy-start.2
  2.0 0.0 copy-start.3
  2.0 0.0 copy-done.2
  2.0 0.6 %copy-done.3 = s32[80]{0:T(128)S(1)} copy-done((s32[80]{0:T(128)S(1)}, s32[80]{0:T(128)}, u32[]{:S(2)}) %copy-start.3) | copy-done | bytes 344
  2.6 0.0 copy-start
  2.6 0.8 %copy-done = f32[10,8,80]{2,1,0:T(8,128)S(1)} copy-done((f32[10,8,80]{2,1,0:T(8,128)S(1)}, f32[10,8,80]{2,1,0:T(8,128)}, u32[]{:S(2)}) %copy-start) | copy-done | bytes 25624
  3.4 0.0 copy-start.1
  3.4 0.7 %copy-done.1 = f32[4,1,10,80]{3,1,2,0:T(1,128)S(1)} copy-done((f32[4,1,10,80]{3,1,2,0:T(1,128)S(1)}, f32[4,1,10,80]{3,1,2,0:T(1,128)}, u32[]{:S(2)}) %copy-start.1) | copy-done | bytes 12824
  4.1 14.4 %shard_map.73 = f32[8,2,10,1,80]{4,3,2,1,0:T(1,128)S(1)} custom-call(f32[4,10,1,80]{3,2,1,0:T(1,128)S(1)} %bitcast.4, f32[10,8,80]{2,1,0:T(8,128)S(1)} %copy-done, s32[1,80]{1,0:T(1,128)S(1)} %bitcast.5, f32[1]{0:T(128)S(6)} %copy.9.sine_ref, f32[1]{0:T(128)S(6)} %copy.10.weight_ref, f32[1]{0:T(128)S(6)} %copy.11.thick_ref, f32[8,1,1,160]{3,2,1,0:T(1,128)S(1)} %copy-done.2), custom_call_target="tpu_custom_call" | custom-call | tf_op jit(solution)/shard_map/pallas_call | solution.py:439
  18.6 0.6 %copy.12 = f32[8,2,1,10,80]{4,2,3,1,0:T(1,128)} copy(f32[8,2,1,10,80]{4,2,3,1,0:T(1,128)S(1)} %bitcast.3) | data formatting | bytes 102400
Async XLA Ops:
  0.0 2.0 %copy-start.2 = (f32[8,1,1,160]{3,2,1,0:T(1,128)S(1)}, f32[8,1,1,160]{3,2,1,0:T(1,128)}, u32[]{:S(2)}) copy-start(f32[8,1,1,160]{3,2,1,0:T(1,128)} %q_ref.1) | copy-start | bytes 15364
  2.0 0.7 %copy-start.3 = (s32[80]{0:T(128)S(1)}, s32[80]{0:T(128)}, u32[]{:S(2)}) copy-start(s32[80]{0:T(128)} %param.9) | copy-start | bytes 964
  2.6 0.8 %copy-start = (f32[10,8,80]{2,1,0:T(8,128)S(1)}, f32[10,8,80]{2,1,0:T(8,128)}, u32[]{:S(2)}) copy-start(f32[10,8,80]{2,1,0:T(8,128)} %leg_ref.1) | copy-start | bytes 76804
  3.4 0.7 %copy-start.1 = (f32[4,1,10,80]{3,1,2,0:T(1,128)S(1)}, f32[4,1,10,80]{3,1,2,0:T(1,128)}, u32[]{:S(2)}) copy-start(f32[4,1,10,80]{3,1,2,0:T(1,128)} %param.7) | copy-start | bytes 38404

commit v4 on v3

--- a/solution.py
+++ b/solution.py
@@ -72,22 +72,22 @@
 
     barrier = pltpu.get_barrier_semaphore()
 
-    def greet(d):
+    def greet_wave(d):
         pl.semaphore_signal(
-            barrier,
-            inc=1,
-            device_id={
-                "wave": lax.rem(me + (d + 1) % n, n),
-                "lev": lax.rem(lev + (d + 1) // n, levels),
-            },
-            device_id_type=MESH,
-        )
-
-    each(n * levels - 1, greet)
+            barrier, inc=1, device_id={"wave": lax.rem(me + d + 1, n)}, device_id_type=MESH
+        )
+
+    def greet_lev(d):
+        pl.semaphore_signal(
+            barrier, inc=1, device_id={"lev": lax.rem(lev + d + 1, levels)}, device_id_type=MESH
+        )
+
+    each(levels - 1, greet_lev)
+    each(n - 1, greet_wave)
 
     vdp[...] = jnp.zeros_like(vdp)
     for f in range(4):
-        vdp[f, :slots, :degrees] = vd_ref[f, :, 0]
+        vdp[f, :slots, :degrees] = vd_ref[f, 0]
     qs[...] = q_ref[:, 0, 0, :]
     owner = owner_ref[...].astype(jnp.float32)
     total_slots = owner.shape[1]
@@ -152,9 +152,8 @@
         east, north, div = fourier[part], fourier[2 + part], fourier[4 + part]
         for t, value in enumerate((east, row_before(north), row_after(north), div)):
             msg[:, 4 * part + t, :] = value
-        dmsg[:, part, :] = div * thick
-
-    pl.semaphore_wait(barrier, n * levels - 1)
+
+    pl.semaphore_wait(barrier, n + levels - 2)
 
     def wave_copy(source, target, send, recv, d, buffer_at, out_at):
         return pltpu.make_async_remote_copy(
@@ -170,22 +169,6 @@
         return wave_copy(msg, recv1, ss1, rs1, d, lax.rem(me + d + 1, n), me)
 
     each(n - 1, lambda d: first(d).start())
-
-    def mass(k):
-        up, to = k // n, k % n
-
-        @pl.when(lev + up + 1 < levels)
-        def _():
-            pltpu.make_async_remote_copy(
-                src_ref=dmsg.at[to],
-                dst_ref=recvd.at[lev, me],
-                send_sem=ssd.at[up],
-                recv_sem=rsd.at[up],
-                device_id={"wave": to, "lev": lev + up + 1},
-                device_id_type=MESH,
-            ).start()
-
-    each((levels - 1) * n, mass)
 
     halos = (
         ("wave", me, n, 1, 0),
@@ -277,6 +260,49 @@
     each(n - 1, first_wait)
     got = jnp.sum(recv1[...], axis=0)
 
+    dmsg[0:1, :] = got[3:4] * thick
+    dmsg[1:2, :] = got[7:8] * thick
+
+    def mass(d):
+        return pltpu.make_async_remote_copy(
+            src_ref=dmsg,
+            dst_ref=recvd.at[lev],
+            send_sem=ssd.at[d],
+            recv_sem=rsd.at[d],
+            device_id={"lev": lev + d + 1},
+            device_id_type=MESH,
+        )
+
+    def mass_start(d):
+        @pl.when(lev + d + 1 < levels)
+        def _():
+            mass(d).start()
+
+    each(levels - 1, mass_start)
+    left = jnp.concatenate([got[0:4], got[4:8]], axis=1)
+    grid = split_dot(left, thigh[...], tlow[...], ((1,), (1,)))
+    q = qs[...]
+    lon_step = 2.0 * math.pi / length
+    lat_step = math.pi / (slots * n)
+    flux = grid[0:1] * q
+    ahead = jnp.concatenate([flux[:, 1:], flux[:, :1]], axis=1)
+    behind = jnp.concatenate([flux[:, -1:], flux[:, :-1]], axis=1)
+    zonal = (ahead - behind) * (1.0 / (2.0 * lon_step))
+
+    for axis, place, count, step, k in halos:
+
+        @pl.when(sends(place, count, -step))
+        def _():
+            halo_copy(axis, place, -step, k).wait_recv()
+
+    merid = (grid[2:3] * qn[1] - grid[1:2] * qn[0]) * (1.0 / (2.0 * lat_step))
+    sine = sine_ref[...].reshape(1, 1)
+    base = (zonal + merid) / (1.0 - sine * sine)
+    layer = grid[3:4] * thick
+    above = qn[2]
+    below = qn[3]
+
+
     def mass_wait(d):
         @pl.when(lev - d - 1 >= 0)
         def _():
@@ -290,37 +316,9 @@
             ).wait_recv()
 
     each(levels - 1, mass_wait)
-    higher = jnp.sum(jnp.sum(recvd[...], axis=0), axis=0)
-    left = jnp.concatenate(
-        [
-            jnp.concatenate([got[0:4], higher[0:1], jnp.zeros((3, wl), jnp.float32)], axis=0),
-            jnp.concatenate([got[4:8], higher[1:2], jnp.zeros((3, wl), jnp.float32)], axis=0),
-        ],
-        axis=1,
-    )
-    grid = split_dot(left, thigh[...], tlow[...], ((1,), (1,)))
-    q = qs[...]
-    lon_step = 2.0 * math.pi / length
-    lat_step = math.pi / (slots * n)
-    flux = grid[0:1] * q
-    ahead = jnp.concatenate([flux[:, 1:], flux[:, :1]], axis=1)
-    behind = jnp.concatenate([flux[:, -1:], flux[:, :-1]], axis=1)
-    zonal = (ahead - behind) * (1.0 / (2.0 * lon_step))
-
-    for axis, place, count, step, k in halos:
-
-        @pl.when(sends(place, count, -step))
-        def _():
-            halo_copy(axis, place, -step, k).wait_recv()
-
-    merid = (grid[2:3] * qn[1] - grid[1:2] * qn[0]) * (1.0 / (2.0 * lat_step))
-    sine = sine_ref[...].reshape(1, 1)
-    base = (zonal + merid) / (1.0 - sine * sine)
-    layer = grid[3:4] * thick
-    above = qn[2]
-    below = qn[3]
-
-    prefix = grid[4:5]
+    higher = jnp.sum(recvd[...], axis=0)
+    left = jnp.concatenate([higher[0:1], higher[1:2]], axis=1)
+    prefix = split_dot(left, thigh[...], tlow[...], ((1,), (1,)))
     omega_bottom = -(prefix + layer)
     omega_top = -prefix
     vertical = (omega_bottom * (q + below) * 0.5 - omega_top * (above + q) * 0.5) / thick
@@ -388,14 +386,7 @@
     def mass_sent(d):
         @pl.when(lev + d + 1 < levels)
         def _():
-            pltpu.make_async_remote_copy(
-                src_ref=dmsg,
-                dst_ref=recvd.at[lev],
-                send_sem=ssd.at[d],
-                recv_sem=rsd.at[d],
-                device_id={"lev": lev + d + 1},
-                device_id_type=MESH,
-            ).wait_send()
+            mass(d).wait_send()
 
     each(levels - 1, mass_sent)
 
@@ -411,7 +402,7 @@
     f32 = jnp.float32
     bf16 = jnp.bfloat16
     operands = (
-        jnp.transpose(vort_div, (0, 2, 1, 3)),
+        vort_div,
         legendre,
         owner_map.reshape(1, -1),
         lat_sine,
@@ -429,8 +420,8 @@
         ((n, 8, wl), f32),
         ((count, length), f32),
         ((4, count, length), f32),
-        ((n, 2, wl), f32),
-        ((levels, n, 2, wl), f32),
+        ((2, wl), f32),
+        ((levels, 2, wl), f32),
         ((n - 1, 2 * count, wl), f32),
         ((n, 2 * count, wl), f32),
     ]

time: 19.5 us -> 17.1 us (0.88)
  the two profiles are of different devices: /device:TPU:0 before, /device:TPU:9 now
where the time goes in v4:
time: 17.1 us; the launch traced here: 16.9 us
  Pallas kernels  13.5 us (79%)
  between operations  1.98 us (12%)
  local copies, waits for them, and re-layouts  1.39 us (8%)
    pallas_call x1, Pallas kernels, shards(): pl.pallas_call(functools.partial(kernel, n, levels, (slots, lat, degrees,...  13.5 us
    unnamed x8, local copies, waits for them, and re-layouts  1.39 us

profile of v4, /device:TPU:9, one launch (start us, length us, event | category | flops | bytes accessed | tf_op | source)
XLA Modules:
  0.0 16.9 jit_solution(2520786831536526268)
XLA Ops:
  0.0 0.0 copy-start
  2.0 0.0 copy-start.1
  2.0 0.0 copy-start.2
  2.0 0.7 %copy.8.vd_ref = f32[4,1,10,80]{3,2,1,0:T(8,128)S(1)} copy(f32[4,1,10,80]{3,1,2,0:T(1,128)} %param.7) | data formatting | bytes 25600 | tf_op args[0]
  2.7 0.0 copy-done
  2.7 0.0 copy-done.1
  2.7 0.0 copy-done.2
  2.7 13.5 %shard_map.73 = f32[8,2,10,1,80]{4,3,2,1,0:T(1,128)S(1)} custom-call(f32[4,1,10,80]{3,2,1,0:T(8,128)S(1)} %copy.8.vd_ref, f32[10,8,80]{2,1,0:T(8,128)S(1)} %copy-done, s32[1,80]{1,0:T(1,128)S(1)} %bitcast.3, f32[1]{0:T(128)S(6)} %copy.10.sine_ref, f32[1]{0:T(128)S(6)} %copy.11.weight_ref, f32[1]{0:T(128)S(6)} %copy.12.thick_ref, f32[8,1,1,160]{3,2,1,0:T(1,128)S(1)} %copy-done.1), custom_call_target="tpu_custom_call" | custom-call | tf_op jit(solution)/shard_map/pallas_call | solution.py:430
  16.2 0.6 %copy.13 = f32[8,2,1,10,80]{4,2,3,1,0:T(1,128)} copy(f32[8,2,1,10,80]{4,2,3,1,0:T(1,128)S(1)} %bitcast.2) | data formatting | bytes 102400
Async XLA Ops:
  0.0 2.7 %copy-start = (f32[10,8,80]{2,1,0:T(8,128)S(1)}, f32[10,8,80]{2,1,0:T(8,128)}, u32[]{:S(2)}) copy-start(f32[10,8,80]{2,1,0:T(8,128)} %leg_ref.1) | copy-start | bytes 76804
  2.0 0.8 %copy-start.1 = (f32[8,1,1,160]{3,2,1,0:T(1,128)S(1)}, f32[8,1,1,160]{3,2,1,0:T(1,128)}, u32[]{:S(2)}) copy-start(f32[8,1,1,160]{3,2,1,0:T(1,128)} %q_ref.1) | copy-start | bytes 15364
  2.0 0.8 %copy-start.2 = (s32[80]{0:T(128)S(1)}, s32[80]{0:T(128)}, u32[]{:S(2)}) copy-start(s32[80]{0:T(128)} %param.9) | copy-start | bytes 964

commit v5 on v4

--- a/solution.py
+++ b/solution.py
@@ -96,7 +96,7 @@
     own_order = jnp.sum(
         jnp.where(place_at == me * slots + slot_at, owner, 0.0), axis=1, keepdims=True
     )
-    thick = thick_ref[...].reshape(1, 1)
+    thick = jnp.full((1, 1), thick_ref[0], jnp.float32)
     sub = lax.broadcasted_iota(jnp.int32, (sp, nd), 0)
     degree = lax.broadcasted_iota(jnp.int32, (sp, nd), 1).astype(jnp.float32)
     order = jnp.where(sub < slots, own_order, 0.0)
@@ -296,7 +296,7 @@
             halo_copy(axis, place, -step, k).wait_recv()
 
     merid = (grid[2:3] * qn[1] - grid[1:2] * qn[0]) * (1.0 / (2.0 * lat_step))
-    sine = sine_ref[...].reshape(1, 1)
+    sine = jnp.full((1, 1), sine_ref[0], jnp.float32)
     base = (zonal + merid) / (1.0 - sine * sine)
     layer = grid[3:4] * thick
     above = qn[2]
@@ -322,7 +322,7 @@
     omega_bottom = -(prefix + layer)
     omega_top = -prefix
     vertical = (omega_bottom * (q + below) * 0.5 - omega_top * (above + q) * 0.5) / thick
-    tendency = -weight_ref[...].reshape(1, 1) * (base + vertical)
+    tendency = -jnp.full((1, 1), weight_ref[0], jnp.float32) * (base + vertical)
 
     spectra = split_dot(tendency, thigh[...], tlow[...], ((1,), (0,))) * (2.0 / length)
     spectra = jnp.concatenate([spectra[:, :wl], spectra[:, wl:]], axis=0)
@@ -430,7 +430,9 @@
     result = pl.pallas_call(
         functools.partial(kernel, n, levels, (slots, lat, degrees, length, count)),
         out_shape=jax.ShapeDtypeStruct((count, 2, slots, 1, degrees), f32),
-        in_specs=[pl.BlockSpec(memory_space=pltpu.VMEM)] * len(operands),
+        in_specs=[
+            pl.BlockSpec(memory_space=pltpu.SMEM if x.shape == (1,) else pltpu.VMEM) for x in operands
+        ],
         out_specs=pl.BlockSpec(memory_space=pltpu.VMEM),
         scratch_shapes=[pltpu.VMEM(shape, kind) for shape, kind in shapes]
         + [dma((n - 1,)), dma((n - 1,)), dma((4,)), dma((4,))]

time: 17.1 us -> 17.1 us (level)
  no operation moved by 1% of the time
where the time goes in v5:
time: 17.1 us; the launch traced here: 16.8 us
  Pallas kernels  13.4 us (78%)
  between operations  1.98 us (12%)
  local copies, waits for them, and re-layouts  1.39 us (8%)
    pallas_call x1, Pallas kernels, shards(): pl.pallas_call(functools.partial(kernel, n, levels, (slots, lat, degrees,...  13.4 us
    unnamed x8, local copies, waits for them, and re-layouts  1.39 us

profile of v5, /device:TPU:9, one launch (start us, length us, event | category | flops | bytes accessed | tf_op | source)
XLA Modules:
  0.0 16.8 jit_solution(13327889941798678906)
XLA Ops:
  0.0 0.0 copy-start
  2.0 0.0 copy-start.1
  2.0 0.0 copy-start.2
  2.0 0.7 %copy.8.vd_ref = f32[4,1,10,80]{3,2,1,0:T(8,128)S(1)} copy(f32[4,1,10,80]{3,1,2,0:T(1,128)} %param.7) | data formatting | bytes 25600 | tf_op args[0]
  2.7 0.0 copy-done
  2.7 0.0 copy-done.1
  2.7 0.0 copy-done.2
  2.7 13.4 %shard_map.73 = f32[8,2,10,1,80]{4,3,2,1,0:T(1,128)S(1)} custom-call(f32[4,1,10,80]{3,2,1,0:T(8,128)S(1)} %copy.8.vd_ref, f32[10,8,80]{2,1,0:T(8,128)S(1)} %copy-done, s32[1,80]{1,0:T(1,128)S(1)} %bitcast.3, f32[1]{0:T(128)S(6)} %copy.10.sine_ref, f32[1]{0:T(128)S(6)} %copy.11.weight_ref, f32[1]{0:T(128)S(6)} %copy.12.thick_ref, f32[8,1,1,160]{3,2,1,0:T(1,128)S(1)} %copy-done.1), custom_call_target="tpu_custom_call" | custom-call | tf_op jit(solution)/shard_map/pallas_call | solution.py:430
  16.2 0.6 %copy.13 = f32[8,2,1,10,80]{4,2,3,1,0:T(1,128)} copy(f32[8,2,1,10,80]{4,2,3,1,0:T(1,128)S(1)} %bitcast.2) | data formatting | bytes 102400
Async XLA Ops:
  0.0 2.7 %copy-start = (f32[10,8,80]{2,1,0:T(8,128)S(1)}, f32[10,8,80]{2,1,0:T(8,128)}, u32[]{:S(2)}) copy-start(f32[10,8,80]{2,1,0:T(8,128)} %leg_ref.1) | copy-start | bytes 76804
  2.0 0.8 %copy-start.1 = (f32[8,1,1,160]{3,2,1,0:T(1,128)S(1)}, f32[8,1,1,160]{3,2,1,0:T(1,128)}, u32[]{:S(2)}) copy-start(f32[8,1,1,160]{3,2,1,0:T(1,128)} %q_ref.1) | copy-start | bytes 15364
  2.0 0.8 %copy-start.2 = (s32[80]{0:T(128)S(1)}, s32[80]{0:T(128)}, u32[]{:S(2)}) copy-start(s32[80]{0:T(128)} %param.9) | copy-start | bytes 964

commit v6 on v5

--- a/solution.py
+++ b/solution.py
@@ -325,18 +325,24 @@
     tendency = -jnp.full((1, 1), weight_ref[0], jnp.float32) * (base + vertical)
 
     spectra = split_dot(tendency, thigh[...], tlow[...], ((1,), (0,))) * (2.0 / length)
-    spectra = jnp.concatenate([spectra[:, :wl], spectra[:, wl:]], axis=0)
+    half = n // 2
+    lane2 = lax.broadcasted_iota(jnp.int32, (tracers, wl), 1)
+    row_of = lax.rem(lane2, n)
+
+    def packed(to):
+        cosine = pltpu.roll(spectra[:, :wl], lax.rem(wl + me - to, wl), 1)
+        sine = pltpu.roll(spectra[:, wl:], lax.rem(wl + lax.rem(me + half, n) - to, wl), 1)
+        return jnp.where(row_of == me, cosine, sine)
 
     def second(d):
         return wave_copy(send2, recv2, ss2, rs2, d, d, me)
 
     def second_start(d):
-        shift = lax.rem(wl + me - lax.rem(me + d + 1, n), wl)
-        send2[d] = pltpu.roll(spectra, shift, 1)
+        send2[d] = packed(lax.rem(me + d + 1, n))
         second(d).start()
 
     each(n - 1, second_start)
-    recv2[me] = spectra
+    recv2[me] = packed(me)
 
     def second_wait(d):
         source = lax.rem(me - d - 1 + n, n)
@@ -350,16 +356,24 @@
         ).wait_recv()
 
     each(n - 1, second_wait)
-    lane2 = lax.broadcasted_iota(jnp.int32, (2 * tracers, wl), 1)
-    row_of = lax.rem(lane2, n)
-    gathered = jnp.zeros((2 * tracers, wl), jnp.float32)
+
+    def gather(i, held):
+        got_cos, got_sin = held
+        piece = recv2[i]
+        return (
+            jnp.where(row_of == i, piece, got_cos),
+            jnp.where(row_of == (i + half) % n, piece, got_sin),
+        )
+
+    parts = (jnp.zeros((tracers, wl), jnp.float32),) * 2
     if n <= 16:
         for i in range(n):
-            gathered = jnp.where(row_of == i, recv2[i], gathered)
+            parts = gather(i, parts)
     else:
-        gathered = lax.fori_loop(
-            0, n, lambda i, g: jnp.where(row_of == i, recv2[i], g), gathered
-        )
+        parts = lax.fori_loop(0, n, gather, parts)
+    got_cos, got_sin = parts
+    got_sin = jnp.where(row_of < half, pltpu.roll(got_sin, wl - half, 1), pltpu.roll(got_sin, half, 1))
+    gathered = jnp.concatenate([got_cos, got_sin], axis=0)
     lane3 = lax.broadcasted_iota(jnp.int32, (sp, wl), 1)
     sub3 = lax.broadcasted_iota(jnp.int32, (sp, wl), 0)
     own = (lane3 >= sub3 * n) & (lane3 < sub3 * n + n)
@@ -395,7 +409,7 @@
     slots, lat, degrees = legendre.shape
     count, own_levels, own_rows, length = tracers.shape
     n, levels = lax.axis_size("wave"), lax.axis_size("lev")
-    assert own_levels == 1 and own_rows == 1 and lat == n
+    assert own_levels == 1 and own_rows == 1 and lat == n and n % 2 == 0
     wl = up_to(slots * n, 128)
     nd = up_to(degrees, 128)
     sp = up_to(slots, 8)
@@ -422,8 +436,8 @@
         ((4, count, length), f32),
         ((2, wl), f32),
         ((levels, 2, wl), f32),
-        ((n - 1, 2 * count, wl), f32),
-        ((n, 2 * count, wl), f32),
+        ((n - 1, count, wl), f32),
+        ((n, count, wl), f32),
     ]
     dma = pltpu.SemaphoreType.DMA
     scratch_bytes = sum(4 * math.prod(shape) for shape, _ in shapes)

time: 17.1 us -> 17 us (level)
  no operation moved by 1% of the time
where the time goes in v6:
time: 17 us; the launch traced here: 16.8 us
  Pallas kernels  13.4 us (79%)
  between operations  1.98 us (12%)
  local copies, waits for them, and re-layouts  1.39 us (8%)
    pallas_call x1, Pallas kernels, shards(): pl.pallas_call(functools.partial(kernel, n, levels, (slots, lat, degrees,...  13.4 us
    unnamed x8, local copies, waits for them, and re-layouts  1.39 us

profile of v6, /device:TPU:9, one launch (start us, length us, event | category | flops | bytes accessed | tf_op | source)
XLA Modules:
  0.0 16.8 jit_solution(3595833391894011696)
XLA Ops:
  0.0 0.0 copy-start
  2.0 0.0 copy-start.1
  2.0 0.0 copy-start.2
  2.0 0.7 %copy.8.vd_ref = f32[4,1,10,80]{3,2,1,0:T(8,128)S(1)} copy(f32[4,1,10,80]{3,1,2,0:T(1,128)} %param.7) | data formatting | bytes 25600 | tf_op args[0]
  2.7 0.0 copy-done
  2.7 0.0 copy-done.1
  2.7 0.0 copy-done.2
  2.7 13.4 %shard_map.73 = f32[8,2,10,1,80]{4,3,2,1,0:T(1,128)S(1)} custom-call(f32[4,1,10,80]{3,2,1,0:T(8,128)S(1)} %copy.8.vd_ref, f32[10,8,80]{2,1,0:T(8,128)S(1)} %copy-done, s32[1,80]{1,0:T(1,128)S(1)} %bitcast.3, f32[1]{0:T(128)S(6)} %copy.10.sine_ref, f32[1]{0:T(128)S(6)} %copy.11.weight_ref, f32[1]{0:T(128)S(6)} %copy.12.thick_ref, f32[8,1,1,160]{3,2,1,0:T(1,128)S(1)} %copy-done.1), custom_call_target="tpu_custom_call" | custom-call | tf_op jit(solution)/shard_map/pallas_call | solution.py:444
  16.1 0.6 %copy.13 = f32[8,2,1,10,80]{4,2,3,1,0:T(1,128)} copy(f32[8,2,1,10,80]{4,2,3,1,0:T(1,128)S(1)} %bitcast.2) | data formatting | bytes 102400
Async XLA Ops:
  0.0 2.7 %copy-start = (f32[10,8,80]{2,1,0:T(8,128)S(1)}, f32[10,8,80]{2,1,0:T(8,128)}, u32[]{:S(2)}) copy-start(f32[10,8,80]{2,1,0:T(8,128)} %leg_ref.1) | copy-start | bytes 76804
  2.0 0.8 %copy-start.1 = (f32[8,1,1,160]{3,2,1,0:T(1,128)S(1)}, f32[8,1,1,160]{3,2,1,0:T(1,128)}, u32[]{:S(2)}) copy-start(f32[8,1,1,160]{3,2,1,0:T(1,128)} %q_ref.1) | copy-start | bytes 15364
  2.0 0.8 %copy-start.2 = (s32[80]{0:T(128)S(1)}, s32[80]{0:T(128)}, u32[]{:S(2)}) copy-start(s32[80]{0:T(128)} %param.9) | copy-start | bytes 964
